TPU v7x, 32 devices: a whole 2x2x4 slice. The times are simulated.
32 devices in a mesh: dp: 4 (over x, core), cent: 8 (over z, y).
Axes of the slice: x: 2, y: 2, z: 4, core: 2. Of those that a mesh axis runs over, the one named last changes fastest.
Arguments:
- embeddings: bfloat16 [8192, 768], P('dp'), may hold values from -40 to 40
- centroids: float32 [8192, 768], P('cent'), may hold values from -0.5 to 0.5
Outputs:
- new_centroids: float32 [8192, 768], P('cent')
- log_total: float32 [8192], P('dp')
All inputs are finite; a program needn't handle non-finite values.
Results may differ from a plain program's by a relative error of at most 0.012.
The roundings to bfloat16 on the way count: a program that leaves them out, or rounds other values in their place, can miss the bound.
Values sent between devices are 32-bit elements; how exact they have to be, the bound alone decides.
No kernel may reach another device: no remote copies, remote signals or barrier semaphores. Data moves between devices by JAX's collectives and lax.ppermute only.
A program may use at most 64 MiB of HBM per device.

v0:
```python
import jax
import jax.numpy as jnp
from jax import lax
from jax.sharding import PartitionSpec as P

ITERS = 2


logit_divisor = 0.05
prior = 0.5


def local(embeddings, centroids):
    current = centroids
    log_total = jnp.zeros((embeddings.shape[0],), jnp.float32)
    for step in range(ITERS):
        rounded = current.astype(jnp.bfloat16)
        pairwise_dots = jnp.dot(embeddings, rounded.T, preferred_element_type=jnp.float32)
        semi_length_energy = 0.5 * jnp.sum(current * current, axis=1)
        cluster_logits = (pairwise_dots - semi_length_energy[None, :]) / logit_divisor
        row_max = lax.pmax(jnp.max(cluster_logits, axis=1), "cent")
        row_total = lax.psum(jnp.sum(jnp.exp(cluster_logits - row_max[:, None]), axis=1), "cent")
        weights = (jnp.exp(cluster_logits - row_max[:, None]) / row_total[:, None]).astype(
            jnp.bfloat16
        )
        sums = lax.dot_general(
            weights, embeddings, (((0,), (0,)), ((), ())), preferred_element_type=jnp.float32
        )
        mass = jnp.sum(weights, axis=0, dtype=jnp.float32)
        sums, mass = lax.psum((sums, mass), "dp")
        current = (sums + prior * current) / (mass + prior)[:, None]
        log_total = row_max + jnp.log(row_total)
    return (current, log_total)


def solution(mesh):
    placed = (P("dp", None), P("cent", None))
    return jax.shard_map(
        local, mesh=mesh, in_specs=placed, out_specs=(P("cent", None), P("dp")), check_vma=False
    )
```

profile of v0, /device:TPU:0, one launch (start us, length us, event | category | flops | bytes accessed | tf_op | source)
XLA Modules:
  0.0 280.8 jit_solution(300629987738442605)
XLA Ops:
  7.2 0.0 copy-start
  7.2 0.0 all-reduce.3.cloned.1.call-start
  7.2 2.3 multiply_reduce_fusion.1
  9.6 0.5 copy-done
  10.0 7.5 %fusion = (f32[2048]{0:T(1024)S(1)}, f32[2048,1024]{0,1:T(8,128)}) fusion(f32[1024]{0:T(1024)S(1)} %broadcast_multiply_fusion.1, bf16[2048,768]{1,0:T(8,128)(2,1)S(1)} %copy-done, f32[1024,768]{1,0:T(8,128)} %param.3), kind=kOutput, calls=%fused_computation.8 | convolution fusion | flops 3228301312 | bytes 14692352 | tf_op jit(solution)/shard_map/dot_general | solution.py:18
  17.5 23.3 %pmax.14 = f32[2048]{0:T(1024)S(1)} all-reduce(f32[2048]{0:T(1024)S(1)} %get-tuple-element.8), channel_id=1, replica_groups=mesh['dp'=4,'cent'=8] {'cent'}, use_global_device_ids=true, to_apply=%region_2.0 | all-reduce | flops 2048 | bytes 16384 | tf_op jit(solution)/shard_map/pmax | solution.py:21
  40.9 4.5 %fusion.2 = f32[2048]{0:T(1024)S(1)} fusion(f32[2048,1024]{0,1:T(8,128)} %get-tuple-element.9, f32[2048]{0:T(1024)S(1)} %pmax.14, f32[1024]{0:T(1024)S(1)} %broadcast_multiply_fusion.1), kind=kLoop, calls=%fused_computation.10 | loop fusion | flops 8386560 | bytes 8409088 | tf_op jit(solution)/shard_map/reduce_sum | solution.py:22
  45.4 17.4 %psum.42 = f32[2048]{0:T(1024)S(1)} all-reduce(f32[2048]{0:T(1024)S(1)} %fusion.2), channel_id=1, replica_groups=mesh['dp'=4,'cent'=8] {'cent'}, use_global_device_ids=true, to_apply=%region_4.0 | all-reduce | flops 2048 | bytes 16384 | tf_op jit(solution)/shard_map/psum | solution.py:22
  62.8 4.7 %convert_reduce_fusion.1 = (f32[1024]{0:T(1024)S(1)}, bf16[2048,1024]{0,1:T(8,128)(2,1)S(1)}) fusion(f32[2048]{0:T(1024)S(1)} %psum.42, f32[2048]{0:T(1024)S(1)} %pmax.14, f32[2048,1024]{0,1:T(8,128)} %get-tuple-element.9, f32[1024]{0:T(1024)S(1)} %broadcast_multiply_fusion.1), kind=kLoop, calls=%fused_computation.4 | loop fusion | flops 14679040 | bytes 12607488 | tf_op jit(solution)/shard_map/reduce_sum | solution.py:29
  67.5 5.1 %fusion.8 = f32[1024,768]{1,0:T(8,128)} fusion(bf16[2048,1024]{0,1:T(8,128)(2,1)S(1)} %get-tuple-element.7, bf16[2048,768]{1,0:T(8,128)(2,1)S(1)} %copy-done), kind=kOutput, calls=%fused_computation.25 | convolution fusion | flops 3221225472 | bytes 10485760 | tf_op jit(solution)/shard_map/dot_general | solution.py:26
  72.6 0.0 all-reduce.3.cloned.1.call-update
  72.6 0.0 all-reduce.5.cloned.1.call-start
  72.7 5.7 %psum.44 = f32[1024]{0:T(1024)S(1)} all-reduce(f32[1024]{0:T(1024)S(1)} %get-tuple-element.6), channel_id=1, replica_groups=mesh['dp'=4,'cent'=8] {'dp'}, use_global_device_ids=true, to_apply=%region_7.0 | all-reduce | flops 1024 | bytes 8192 | tf_op jit(solution)/shard_map/psum | solution.py:30
  78.4 61.6 %all-reduce.3.cloned.1.call-done = f32[1024,768]{1,0:T(8,128)} async-done(((f32[1024,768]{1,0:T(8,128)}), f32[1024,768]{1,0:T(8,128)}) %all-reduce.3.cloned.1.call-update) | async-done | bytes 3145744 | tf_op jit(solution)/shard_map/psum | solution.py:30
  139.9 3.5 %multiply_reduce_fusion = (f32[1024]{0:T(1024)S(1)}, f32[1024,768]{1,0:T(8,128)S(1)}) fusion(f32[1024]{0:T(1024)S(1)} %broadcast_add_fusion.1, f32[1024,768]{1,0:T(8,128)} %all-reduce.3.cloned.1.call-done, f32[1024,768]{1,0:T(8,128)} %param.3), kind=kLoop, calls=%fused_computation.13 | loop fusion | flops 3931136 | bytes 9445376 | tf_op jit(solution)/shard_map/reduce_sum | solution.py:19
  143.4 0.0 copy-start.1
  143.4 5.7 %fusion.1 = (f32[2048]{0:T(1024)S(1)}, f32[1024,2048]{1,0:T(8,128)}) fusion(f32[1024]{0:T(1024)S(1)} %broadcast_multiply_fusion, bf16[2048,768]{1,0:T(8,128)(2,1)S(1)} %copy-done, f32[1024,768]{1,0:T(8,128)S(1)} %get-tuple-element.5), kind=kOutput, calls=%fused_computation.9 | convolution fusion | flops 3228301312 | bytes 14692352 | tf_op jit(solution)/shard_map/dot_general | solution.py:18
  149.1 0.0 copy-done.1
  149.1 21.6 %pmax.15 = f32[2048]{0:T(1024)S(1)} all-reduce(f32[2048]{0:T(1024)S(1)} %get-tuple-element.10), channel_id=1, replica_groups=mesh['dp'=4,'cent'=8] {'cent'}, use_global_device_ids=true, to_apply=%region_10.0 | all-reduce | flops 2048 | bytes 16384 | tf_op jit(solution)/shard_map/pmax | solution.py:21
  170.7 4.5 %fusion.3 = f32[2048]{0:T(1024)S(1)} fusion(f32[1024,2048]{1,0:T(8,128)} %get-tuple-element.11, f32[2048]{0:T(1024)S(1)} %pmax.15, f32[1024]{0:T(1024)S(1)} %broadcast_multiply_fusion), kind=kLoop, calls=%fused_computation.11 | loop fusion | flops 8386560 | bytes 8409088 | tf_op jit(solution)/shard_map/reduce_sum | solution.py:22
  175.2 17.6 %psum.45 = f32[2048]{0:T(1024)S(1)} all-reduce(f32[2048]{0:T(1024)S(1)} %fusion.3), channel_id=1, replica_groups=mesh['dp'=4,'cent'=8] {'cent'}, use_global_device_ids=true, to_apply=%region_12.0 | all-reduce | flops 2048 | bytes 16384 | tf_op jit(solution)/shard_map/psum | solution.py:22
  192.8 4.7 %convert_reduce_fusion = (f32[1024]{0:T(1024)S(1)}, bf16[1024,2048]{1,0:T(8,128)(2,1)S(1)}) fusion(f32[2048]{0:T(1024)S(1)} %psum.45, f32[2048]{0:T(1024)S(1)} %pmax.15, f32[1024,2048]{1,0:T(8,128)} %get-tuple-element.11, f32[1024]{0:T(1024)S(1)} %broadcast_multiply_fusion), kind=kLoop, calls=%fused_computation | loop fusion | flops 14679040 | bytes 12607488 | tf_op jit(solution)/shard_map/reduce_sum | solution.py:29
  197.5 5.1 %fusion.9 = f32[1024,768]{1,0:T(8,128)} fusion(bf16[1024,2048]{1,0:T(8,128)(2,1)S(1)} %get-tuple-element.3, bf16[2048,768]{1,0:T(8,128)(2,1)S(1)} %copy-done), kind=kOutput, calls=%fused_computation.26 | convolution fusion | flops 3221225472 | bytes 10485760 | tf_op jit(solution)/shard_map/dot_general | solution.py:26
  202.6 0.0 all-reduce.5.cloned.1.call-update
  202.6 5.7 %psum.47 = f32[1024]{0:T(1024)S(1)} all-reduce(f32[1024]{0:T(1024)S(1)} %get-tuple-element.2), channel_id=1, replica_groups=mesh['dp'=4,'cent'=8] {'dp'}, use_global_device_ids=true, to_apply=%region_15.0 | all-reduce | flops 1024 | bytes 8192 | tf_op jit(solution)/shard_map/psum | solution.py:30
  208.3 0.6 log_add_fusion
  208.9 60.2 %all-reduce.5.cloned.1.call-done = f32[1024,768]{1,0:T(8,128)} async-done(((f32[1024,768]{1,0:T(8,128)}), f32[1024,768]{1,0:T(8,128)}) %all-reduce.5.cloned.1.call-update) | async-done | bytes 3145744 | tf_op jit(solution)/shard_map/psum | solution.py:30
  269.1 4.9 %add_divide_fusion = f32[1024,768]{1,0:T(8,128)} fusion(f32[1024,768]{1,0:T(8,128)} %all-reduce.5.cloned.1.call-done, f32[1024,768]{1,0:T(8,128)} %copy-done.1, f32[1024]{0:T(1024)S(1)} %broadcast_add_fusion), kind=kLoop, calls=%fused_computation.12 | loop fusion | flops 2359296 | bytes 9441280 | tf_op jit(solution)/shard_map/div | solution.py:31
  (4 shorter events, 0.0 us)
Async XLA Ops:
  7.2 2.8 %copy-start = (bf16[2048,768]{1,0:T(8,128)(2,1)S(1)}, bf16[2048,768]{1,0:T(8,128)(2,1)}, u32[]{:S(2)}) copy-start(bf16[2048,768]{1,0:T(8,128)(2,1)} %param.2) | copy-start | bytes 9437188
  7.2 132.7 %all-reduce.3.cloned.1.call-start = ((), (), s32[]{:S(2)}) async-start(), calls=%async_computation | async-start | bytes 6291456 | tf_op jit(solution)/shard_map/psum | solution.py:30
  72.6 196.5 %all-reduce.5.cloned.1.call-start = ((), (), s32[]{:S(2)}) async-start(), calls=%async_computation.1 | async-start | bytes 6291456 | tf_op jit(solution)/shard_map/psum | solution.py:30
  143.4 5.7 %copy-start.1 = (f32[1024,768]{1,0:T(8,128)}, f32[1024,768]{1,0:T(8,128)S(1)}, u32[]{:S(2)}) copy-start(f32[1024,768]{1,0:T(8,128)S(1)} %get-tuple-element.5) | copy-start | bytes 9437188
Sparse Core Ops, SparseCore 0:
  72.7 67.1 all-reduce.2
  202.8 66.2 all-reduce.4
where the time goes:
time: 281 us
  waiting for transfers between devices  122 us (43%)
  blocking collectives  91.2 us (32%)
  other arithmetic  29.8 us (11%)
  matrix products  23.3 us (8%)
  between operations  14.1 us (5%)
    psum x2, waiting for transfers between devices, local(): sums, mass = lax.psum((sums, mass), 'dp')  122 us
    pmax x2, blocking collectives, local(): row_max = lax.pmax(jnp.max(cluster_logits, axis=1), 'cent')  45 us
    psum x2, blocking collectives, local(): lax.psum(jnp.sum(jnp.exp(cluster_logits - row_max[:, None]), axis=1), 'ce...  34.9 us
    dot_general x2, matrix products, local(): jnp.dot(embeddings, rounded.T, preferred_element_type=jnp.float32)  13.2 us
    psum x2, blocking collectives, local(): sums, mass = lax.psum((sums, mass), 'dp')  11.3 us
    dot_general x2, matrix products, local(): lax.dot_general(weights, embeddings, (((0,), (0,)), ((), ())), preferred_...  10.2 us
    reduce_sum x2, other arithmetic, local(): mass = jnp.sum(weights, axis=0, dtype=jnp.float32)  9.46 us
    reduce_sum x2, other arithmetic, local(): jnp.sum(jnp.exp(cluster_logits - row_max[:, None]), axis=1)  9.01 us
  transfers between devices with their start and end apart: 2, of which 2 were waited for; matrix products, arithmetic and copies ran while one was open for 0% of the time, Pallas kernels for 0%

commit v1 on v0

v1 whole, which is shorter than its diff:
```python
import functools

import jax
import jax.numpy as jnp
import numpy as np
from jax import lax
from jax.experimental import pallas as pl
from jax.experimental.pallas import tpu as pltpu
from jax.sharding import PartitionSpec as P

ITERS = 2
UNITS = (1, 2, 1)
CHUNKS = sum(UNITS)
MASS = 8
PARTS = ((1, 4, 3), (1, 4, 3))
EARLY_PARTS = (4, 4)
TAILS = (1, 1)
ROWS = 512
TILE = 256
AHEAD = 3

logit_divisor = 0.05
prior = 0.5
SCALE = float(np.log2(np.e) / logit_divisor)
LN2 = float(np.log(2.0))

ANY = pl.BlockSpec(memory_space=pl.ANY)
VMEM = pl.BlockSpec(memory_space=pltpu.VMEM)
SMEM = pl.BlockSpec(memory_space=pltpu.SMEM)
HBM = pl.BlockSpec(memory_space=pltpu.HBM)


def call(kernel, name, in_specs, out_specs, out_shapes, scratch=(), limit=12, **more):
    return pl.pallas_call(
        kernel,
        in_specs=in_specs,
        out_specs=out_specs,
        out_shape=[jax.ShapeDtypeStruct(s, d) for s, d in out_shapes],
        scratch_shapes=list(scratch),
        compiler_params=pltpu.CompilerParams(vmem_limit_bytes=limit * 2**20),
        cost_estimate=pl.CostEstimate(flops=1, bytes_accessed=1, transcendentals=0),
        name=name,
        **more,
    )


def prepare(c, cb, energy, at):
    n = c.shape[0]
    cb[at : at + n] = c.astype(jnp.bfloat16)
    half = 0.5 * jnp.sum(c * c, axis=1, keepdims=True)
    energy[at : at + n] = jnp.broadcast_to(half, (n, 128))


def score_tile(cb, energy, turned_ref, r, at, size, s_refs):
    rows = slice(r, r + ROWS)
    dots = jnp.dot(cb[at : at + size], turned_ref[:, rows], preferred_element_type=jnp.float32)
    s = (dots - energy[at : at + size, :1]) * SCALE
    n = s_refs[0].shape[0] // 2
    half = len(s_refs) * n
    for k in range(0, size, n):
        side, c = divmod(at + k, half)
        s_refs[c // n][side * n : (side + 1) * n, rows] = s[k : k + n]
    top = jnp.max(s, axis=0, keepdims=True)
    return top, jnp.sum(jnp.exp2(s - top), axis=0, keepdims=True)


def finish_rows(r, parts, stats_ref, prev_ref):
    rows = slice(r, r + ROWS)
    if prev_ref is not None:
        parts = parts + [(prev_ref[0:1, rows], prev_ref[1:2, rows])]
    top = functools.reduce(jnp.maximum, [m for m, _ in parts])
    stats_ref[0:1, rows] = top
    stats_ref[1:2, rows] = sum(l * jnp.exp2(m - top) for m, l in parts)


def first_kernel(core_ref, c_hbm, emb_hbm, emb_ref, turned_ref, stats_ref, *refs):
    s_refs, old_refs = refs[:CHUNKS], refs[CHUNKS : 2 * CHUNKS]
    theirs, cb, energy, c_sems, emb_sems = refs[2 * CHUNKS :]
    n = old_refs[0].shape[0]
    half = CHUNKS * n
    core = core_ref[0]
    starts = [pl.multiple_of(core * half, half), pl.multiple_of((1 - core) * half, half)]
    blocks = range(0, emb_ref.shape[0], ROWS)
    tiles = range(0, 2 * half, TILE)

    def centroids_of(i, at):
        if at >= half:
            to = theirs.at[pl.ds(at - half, TILE)]
            return [pltpu.make_async_copy(c_hbm.at[pl.ds(starts[1] + at - half, TILE)], to, c_sems.at[CHUNKS + i])]
        return [
            pltpu.make_async_copy(c_hbm.at[pl.ds(starts[0] + c * n, n)], old_refs[c], c_sems.at[c])
            for c in range(at // n, (at + TILE) // n)
        ]

    def rows_of(i, r):
        return [pltpu.make_async_copy(emb_hbm.at[pl.ds(r, ROWS)], emb_ref.at[pl.ds(r, ROWS)], emb_sems.at[i])]

    groups = []
    for i in range(max(len(blocks), len(tiles))):
        groups.append((blocks[i : i + 1], [(t, tiles[t]) for t in (i,) if t < len(tiles)]))
    copies = [
        [copy for r in rows for copy in rows_of(i, r)] + [copy for t, at in new for copy in centroids_of(t, at)]
        for i, (rows, new) in enumerate(groups)
    ]
    for group in copies[:AHEAD]:
        for copy in group:
            copy.start()
    have_rows, have_tiles, parts = [], [], {r: [] for r in blocks}
    for i, (new_rows, new_tiles) in enumerate(groups):
        for copy in copies[i]:
            copy.wait()
        for group in copies[i + AHEAD : i + AHEAD + 1]:
            for copy in group:
                copy.start()
        for r in new_rows:
            turned_ref[:, r : r + ROWS] = emb_ref[r : r + ROWS].T
        for _, at in new_tiles:
            if at < half:
                for c in range(at // n, (at + TILE) // n):
                    prepare(old_refs[c][...], cb, energy, c * n)
            else:
                prepare(theirs[at - half : at - half + TILE], cb, energy, at)
        todo = [(r, at) for r in new_rows for at in have_tiles]
        have_rows += new_rows
        todo += [(r, at) for _, at in new_tiles for r in have_rows]
        have_tiles += [at for _, at in new_tiles]
        for r, at in todo:
            parts[r].append(score_tile(cb, energy, turned_ref, r, at, TILE, s_refs))
            if len(parts[r]) == len(tiles):
                finish_rows(r, parts[r], stats_ref, None)


def first_call(core, centroids, embeddings):
    rows, width = embeddings.shape
    count = centroids.shape[0]
    f32, bf16 = jnp.float32, jnp.bfloat16
    emb, turned, stats, *out = call(
        first_kernel, "first_scores", [SMEM, HBM, HBM], [VMEM] * (3 + 2 * CHUNKS),
        [((rows, width), bf16), ((width, rows), bf16), ((2, rows), f32)]
        + [((count // CHUNKS, rows), f32)] * CHUNKS
        + [((count // CHUNKS // 2, width), f32)] * CHUNKS,
        [pltpu.VMEM((count // 2, width), f32), pltpu.VMEM((count, width), bf16), pltpu.VMEM((count, 128), f32),
         pltpu.SemaphoreType.DMA((CHUNKS + count // TILE,)), pltpu.SemaphoreType.DMA((rows // ROWS,))],
        limit=37,
    )(core, centroids, embeddings)
    return out[CHUNKS:], emb, turned, stats, out[:CHUNKS]


def scores_kernel(turned_ref, *refs, chained, chunks, pieces):
    c_refs, refs = refs[:pieces], refs[pieces:]
    prev_ref = refs[0] if chained else None
    stats_ref, *s_refs = refs[chained : chained + 1 + chunks]
    cb, energy = refs[chained + 1 + chunks :]
    at = 0
    for ref in c_refs:
        prepare(ref[...], cb, energy, at)
        at += ref.shape[0]
    for r in range(0, turned_ref.shape[1], ROWS):
        size = min(TILE, cb.shape[0])
        parts = [score_tile(cb, energy, turned_ref, r, at, size, s_refs) for at in range(0, cb.shape[0], size)]
        finish_rows(r, parts, stats_ref, prev_ref)


def scores_call(blocks, chunks, turned, prev):
    width, rows = turned.shape
    total = sum(a.shape[0] for a in blocks)
    chained = prev is not None
    stats, *scores = call(
        functools.partial(scores_kernel, chained=chained, chunks=chunks, pieces=len(blocks)),
        "scores", [VMEM] * (1 + len(blocks) + chained), [VMEM] * (1 + chunks),
        [((2, rows), jnp.float32)] + [((total // chunks, rows), jnp.float32)] * chunks,
        [pltpu.VMEM((total, width), jnp.bfloat16), pltpu.VMEM((total, 128), jnp.float32)],
        limit=24,
    )(turned, *blocks, *([prev] if chained else []))
    return stats, scores


def split(rows, parts):
    tiles = rows // 8
    return [8 * (tiles // parts + (i < tiles % parts)) for i in range(parts)]


def put_rows(refs, at, value):
    done = 0
    for ref in refs:
        size = ref.shape[0]
        n = min(size - at, value.shape[0] - done)
        if at < size and n > 0:
            ref[at : at + n] = value[done : done + n]
            done += n
            at = 0
        else:
            at -= size


def weights_of(s_refs, stats_ref, rows):
    scale = 1.0 / stats_ref[1:2, rows]
    s = jnp.concatenate([ref[:, rows] for ref in s_refs], axis=0)
    return (jnp.exp2(s - stats_ref[0:1, rows]) * scale).astype(jnp.bfloat16)


def lane_sums(w):
    wide = w.astype(jnp.float32)
    return sum(wide[:, at : at + 128] for at in range(0, w.shape[1], 128))


def grouped(refs, counts):
    ends = [sum(counts[: i + 1]) for i in range(len(counts))]
    return [refs[end - count : end] for end, count in zip(ends, counts)]


def sums_kernel(stats_ref, emb_ref, *refs, counts, extra, deps):
    scores, refs = grouped(refs, counts), refs[sum(counts) + deps :]
    out_mine, out_theirs, out_masses = refs[:1], refs[1 : len(refs) - 2 * bool(extra)], refs[-2:]
    n = sum(ref.shape[0] for ref in scores[0]) // 2
    blocks = [slice(r, r + ROWS) for r in range(0, emb_ref.shape[0], ROWS)]
    first, last = (extra[0], len(scores) - extra[1]) if extra else (0, len(scores))
    heavies = []
    for u, s_refs in enumerate(scores):
        acc, heavy = None, None
        for rows in blocks:
            w = weights_of(s_refs, stats_ref, rows)
            if first <= u < last:
                part = jnp.dot(w, emb_ref[rows], preferred_element_type=jnp.float32)
                acc = part if acc is None else acc + part
            if extra:
                heavy = lane_sums(w) if heavy is None else heavy + lane_sums(w)
        if first <= u < last:
            put_rows(out_mine, (u - first) * n, acc[:n])
            put_rows(out_theirs, (u - first) * n, acc[n:])
        heavies.append(heavy)
    if not extra:
        return
    eye = lax.broadcasted_iota(jnp.int32, (n, n), 0) == lax.broadcasted_iota(jnp.int32, (n, n), 1)
    for k, out_ref in enumerate(out_masses):
        out_ref[...] = jnp.zeros_like(out_ref)
        for u, heavy in enumerate(heavies):
            column = jnp.sum(heavy[k * n : (k + 1) * n], axis=1, keepdims=True)
            out_ref[u : u + 1] = jnp.sum(jnp.where(eye, column, 0.0), axis=0, keepdims=True)


def sums_call(scores, extra, stats, embeddings, parts, deps):
    units = len(scores) - sum(extra)
    arrays = [a for unit in scores for a in unit]
    n, width = sum(a.shape[0] for a in scores[0]) // 2, embeddings.shape[1]
    shapes = [(size, width) for size in [units * n] + split(units * n, parts)] + [(MASS, n)] * (2 * bool(extra))
    mine, *out = call(
        functools.partial(sums_kernel, counts=tuple(len(unit) for unit in scores), extra=extra, deps=len(deps)),
        "sums", [VMEM] * (2 + len(arrays)) + [ANY] * len(deps), [VMEM] * len(shapes),
        [(shape, jnp.float32) for shape in shapes],
    )(stats, embeddings, *arrays, *deps)
    return mine, out[:parts], out[parts:]


def side_kernel(stats_ref, emb_ref, s_ref, *refs, side, deps):
    n = s_ref.shape[0] // 2
    acc = None
    for r in range(0, emb_ref.shape[0], ROWS):
        rows = slice(r, r + ROWS)
        w = weights_of([s_ref.at[side * n : (side + 1) * n]], stats_ref, rows)
        part = jnp.dot(w, emb_ref[rows], preferred_element_type=jnp.float32)
        acc = part if acc is None else acc + part
    put_rows(refs[deps:], 0, acc)


def side_call(s, side, stats, embeddings, parts, deps):
    n, width = s.shape[0] // 2, embeddings.shape[1]
    return call(
        functools.partial(side_kernel, side=side, deps=len(deps)),
        "side_sums", [VMEM] * 3 + [ANY] * len(deps), [VMEM] * parts,
        [((size, width), jnp.float32) for size in split(n, parts)],
    )(stats, embeddings, s, *deps)


def fold_kernel(mine_ref, *refs, parts, masses):
    came_refs, mass_refs, total_refs = refs[:parts], refs[parts : parts + masses], refs[parts + masses :]
    at = 0
    for ref in came_refs:
        size = ref.shape[0]
        put_rows(total_refs, at, mine_ref[at : at + size] + ref[...])
        at += size
    if masses:
        total = mass_refs[0][...] + mass_refs[1][...]
        rest = jnp.zeros((MASS, mine_ref.shape[1] - total.shape[1]), jnp.float32)
        put_rows(total_refs, at, jnp.concatenate([total, rest], axis=1))


def fold_call(mine, came, units, masses):
    rows, width = mine.shape
    sizes = [rows // units] * units
    sizes[-1] += MASS * bool(masses)
    return call(
        functools.partial(fold_kernel, parts=len(came), masses=len(masses)),
        "fold", [VMEM] * (1 + len(came) + len(masses)), [VMEM] * units,
        [((size, width), jnp.float32) for size in sizes],
    )(mine, *came, *masses)


def update_kernel(*refs, units, first, whole, deps):
    mass_refs, new_refs = refs[3 * units : 3 * units + 2], refs[3 * units + 2 + deps :]
    n = refs[2].shape[0]
    eye = lax.broadcasted_iota(jnp.int32, (n, n), 0) == lax.broadcasted_iota(jnp.int32, (n, n), 1)
    masses = mass_refs[0][n : n + MASS, :n] + mass_refs[1][n : n + MASS, :n]
    for u in range(units):
        own_ref, far_ref, old_ref = refs[3 * u : 3 * u + 3]
        row = masses[first + u : first + u + 1]
        mass = jnp.sum(jnp.where(eye, row, 0.0), axis=1, keepdims=True)
        new = (own_ref[:n] + far_ref[:n] + prior * old_ref[...]) / (mass + prior)
        if whole:
            new_refs[u][...] = new
        put_rows(new_refs[units * whole :], u * n, new)


def update_call(pieces, masses, old, first, parts, whole, deps):
    units = len(old)
    n, width = old[0].shape
    sizes = [n] * units * whole + (split(units * n, parts) if parts else [])
    out = call(
        functools.partial(update_kernel, units=units, first=first, whole=whole, deps=len(deps)),
        "update", [VMEM] * (3 * units + 2) + [ANY] * len(deps), [VMEM] * len(sizes),
        [((size, width), jnp.float32) for size in sizes],
    )(*[a for p, o in zip(pieces, old) for a in (*p, o)], *masses, *deps)
    return out[: units if whole else None], out[units * whole :] or out


def place_kernel(at_ref, *refs, first, counts, given):
    size = sum(counts)
    blocks, out_ref, done_refs, sems = refs[:size], refs[size + given], refs[size + given + 1 : -1], refs[-1]
    copies = []
    for side, part in enumerate((blocks[: counts[0]], blocks[counts[0] :])):
        at = first
        for ref in part:
            n = ref.shape[0]
            to = out_ref.at[pl.ds(pl.multiple_of(at_ref[side] + at, 8), n)]
            copies.append(pltpu.make_async_copy(ref, to, sems.at[len(copies)]))
            at += n
    for copy in copies:
        copy.start()
    for copy in copies:
        copy.wait()
    for ref in done_refs:
        ref[...] = jnp.zeros_like(ref)


def place_call(at, mine, theirs, first, shape, out):
    given = [] if out is None else [out]
    size = len(mine) + len(theirs)
    done = [((8, 128), jnp.float32)] * (out is None)
    return call(
        functools.partial(place_kernel, first=first, counts=(len(mine), len(theirs)), given=len(given)),
        "place", [SMEM] + [VMEM] * size + [HBM] * len(given), [HBM] + [VMEM] * len(done),
        [(shape, jnp.float32)] + done, [pltpu.SemaphoreType.DMA((size,))],
        input_output_aliases={size + 1: 0} if given else {},
    )(at, *mine, *theirs, *given)


def exchange_stats(stats, n_cent):
    spread = jnp.broadcast_to(stats[None], (n_cent, *stats.shape))
    pairs = lax.all_to_all(spread, "cent", 0, 0)
    top = jnp.max(pairs[:, 0], axis=0)
    total = jnp.sum(jnp.exp2((pairs[:, 0] - top) + jnp.log2(pairs[:, 1])), axis=0)
    return jnp.stack([top, total])


def local(embeddings, centroids, n_dp, n_cent):
    core = lax.axis_index("dp") % 2
    half = centroids.shape[0] // 2
    early = CHUNKS - UNITS[-1]
    firsts = [sum(UNITS[:c]) for c in range(len(UNITS))]
    by_core = lambda a: lax.ppermute(a, "dp", [(i, i ^ 1) for i in range(n_dp)])
    by_chip = lambda a: lax.ppermute(a, "dp", [(i, i ^ 2) for i in range(n_dp)])
    old, embeddings, turned, stats, scores = first_call(core.astype(jnp.int32)[None], centroids, embeddings)
    scores = [(s,) for s in scores]
    for step in range(ITERS):
        last = step == ITERS - 1
        stats = exchange_stats(stats, n_cent)
        log_total = (stats[0] + jnp.log2(stats[1])) * LN2
        sums = []
        for c, (first, units) in enumerate(zip(firsts, UNITS)):
            deps = [sums[-1][0]] if c else []
            deps += [sums[0][1]] if c > 1 else []
            if c == 0:
                theirs, masses = side_call(scores[0][0], 1, stats, embeddings, PARTS[step][0], []), []
                (mine,) = side_call(scores[0][0], 0, stats, embeddings, 1, theirs[-1:])
            elif c == 1:
                extra = (first, CHUNKS - first - units)
                mine, theirs, masses = sums_call(scores, extra, stats, embeddings, PARTS[step][c], deps)
            else:
                mine, theirs, masses = sums_call(scores[first:], (), stats, embeddings, PARTS[step][c], deps)
            masses = [masses[0], by_core(masses[1])] if masses else []
            totals = fold_call(mine, [by_core(t) for t in theirs], units, masses)
            sums += [(t, by_chip(t)) for t in totals]
        masses = sums[early - 1]
        deps = [log_total] if last else []
        new, sent = update_call(sums[:early], masses, old[:early], 0, EARLY_PARTS[step], not last, [sums[-1][0]] + deps)
        came = [by_core(a) for a in sent]
        if last:
            ends = jnp.stack([core * half, (1 - core) * half]).astype(jnp.int32)
            out, ready = place_call(ends, new, came, 0, centroids.shape, None)
        else:
            ready, scores = scores_call([*new, *came], early, turned, None)
            scores = [(s,) for s in scores]
        new_last, sent = update_call(sums[early:], masses, old[early:], early, TAILS[step], not last, [ready])
        came_last = [by_core(a) for a in sent]
        if last:
            (out,) = place_call(ends, new_last, came_last, early * half // CHUNKS, centroids.shape, out)
        else:
            stats, own = scores_call(new_last, 1, turned, ready)
            stats, other = scores_call(came_last, 1, turned, stats)
            scores.append((*own, *other))
            old = new + new_last
    return out, log_total


def solution(mesh):
    n_dp, n_cent = mesh.shape["dp"], mesh.shape["cent"]
    placed = (P("dp", None), P("cent", None))
    return jax.shard_map(
        lambda e, c: local(e, c, n_dp, n_cent),
        mesh=mesh, in_specs=placed, out_specs=(P("cent", None), P("dp")), check_vma=False,
    )
```

time: 281 us -> 118 us (0.42)
  waiting for transfers between devices: 122 us -> 48 us
  blocking collectives: 91.2 us -> 24.4 us
  other arithmetic: 29.8 us -> 0.56 us
  Pallas kernels: 0 us -> 26.7 us
  matrix products: 23.3 us -> 0 us
  starting transfers between devices: 0.08 us -> 16.6 us
  between operations: 14.1 us -> 1.11 us
    psum x2 -> x0, waiting for transfers between devices: 122 us -> none  [local(): sums, mass = lax.psum((sums, mass), 'dp')]
    ppermute x0 -> x36, waiting for transfers between devices: none -> 48 us  [the longest x8 34.1 us: local(): by_chip = lambda a: lax.ppermute(a, 'dp', [(i, i ^ 2) for i in range(n_dp)])]
    psum x4 -> x0, blocking collectives: 46.3 us -> none  [the longest x2 34.9 us: local(): lax.psum(jnp.sum(jnp.exp(cluster_logits - row_max[:, None]), axis=1), 'ce...]
    pmax x2 -> x0, blocking collectives: 45 us -> none  [local(): row_max = lax.pmax(jnp.max(cluster_logits, axis=1), 'cent')]
    pallas_call x0 -> x24, Pallas kernels: none -> 26.7 us  [the longest x4 7.43 us: sums_call(): call(functools.partial(sums_kernel, counts=tuple((len(unit) for unit in s...]
    all_to_all x0 -> x2, blocking collectives: none -> 24.4 us  [exchange_stats(): pairs = lax.all_to_all(spread, 'cent', 0, 0)]
    reduce_sum x6 -> x2, other arithmetic: 24.3 us -> 0.15 us  [exchange_stats(): total = jnp.sum(jnp.exp2(pairs[:, 0] - top + jnp.log2(pairs[:, 1])), axis=0)]
    dot_general x4 -> x0, matrix products: 23.3 us -> none  [the longest x2 13.2 us: local(): jnp.dot(embeddings, rounded.T, preferred_element_type=jnp.float32)]
  transfers between devices with their start and end apart: 2 -> 36, of which waited for: 2 -> 32; matrix products, arithmetic and copies ran while one was open for 0% -> 0% of each run, Pallas kernels for 0% -> 14%
where the time goes in v1:
time: 118 us; the launch traced here: 117 us
  waiting for transfers between devices  48 us (41%)
  Pallas kernels  26.7 us (23%)
  blocking collectives  24.4 us (21%)
  starting transfers between devices  16.6 us (14%)
    ppermute x8, waiting for transfers between devices, local(): by_chip = lambda a: lax.ppermute(a, 'dp', [(i, i ^ 2) for i in range(n_dp)])  34.1 us
    all_to_all x2, blocking collectives, exchange_stats(): pairs = lax.all_to_all(spread, 'cent', 0, 0)  24.4 us
    ppermute x28, waiting for transfers between devices, local(): by_core = lambda a: lax.ppermute(a, 'dp', [(i, i ^ 1) for i in range(n_dp)])  14 us
    ppermute x8, starting transfers between devices, local(): by_chip = lambda a: lax.ppermute(a, 'dp', [(i, i ^ 2) for i in range(n_dp)])  10.4 us
    pallas_call x4, Pallas kernels, sums_call(): call(functools.partial(sums_kernel, counts=tuple((len(unit) for unit in s...  7.43 us
    pallas_call x1, Pallas kernels, first_call(): call(first_kernel, 'first_scores', [SMEM, HBM, HBM], [VMEM] * (3 + 2 * CH...  6.75 us
    ppermute x28, starting transfers between devices, local(): by_core = lambda a: lax.ppermute(a, 'dp', [(i, i ^ 1) for i in range(n_dp)])  6.22 us
    pallas_call x3, Pallas kernels, scores_call(): call(functools.partial(scores_kernel, chained=chained, chunks=chunks, pie...  4.85 us
  transfers between devices with their start and end apart: 36, of which 32 were waited for; matrix products, arithmetic and copies ran while one was open for 0% of the time, Pallas kernels for 14%

profile of v1, /device:TPU:0, one launch (start us, length us, event | category | flops | bytes accessed | tf_op | source)
XLA Modules:
  0.0 117.5 jit_solution(1312046322168549724)
XLA Ops:
  0.6 6.7 %first_scores.1 = (bf16[2048,768]{1,0:T(8,128)(2,1)S(1)}, bf16[768,2048]{1,0:T(8,128)(2,1)S(1)}, f32[2,2048]{1,0:T(2,128)S(1)}, f32[256,2048]{1,0:T(8,128)S(1)},...) custom-call(s32[1]{0:T(128)} %bitcast.2.core_ref, ...), custom_call_target="tpu_custom_call" | custom-call | flops 1 | bytes 1 | tf_op jit(solution)/shard_map/first_scores/pallas_call | solution.py:137
  7.4 14.4 %all_to_all.10 = f32[8,2,2048]{2,1,0:T(2,128)S(1)} all-to-all(f32[8,2,2048]{2,1,0:T(2,128)S(1)} %broadcast_in_dim.7), channel_id=1, replica_groups=mesh['dp'=4,'cent'=8] {'cent'}, dimensions={0} | all-to-all | bytes 262144 | tf_op jit(solution)/shard_map/all_to_all | solution.py:359
  23.4 1.1 collective-permute-done.refs_0_
  24.6 1.6 %collective-permute-start.6 = (f32[128,768]{1,0:T(8,128)S(1)}, f32[128,768]{1,0:T(8,128)S(1)}, u32[]{:S(2)}, u32[]{:S(2)}) collective-permute-start(f32[128,768]{1,0:T(8,128)S(1)} %fold.6.refs_4_.refs_0_), channel_id=1, source_target_pairs={{0,16},{8,24},{16,0},{24,8},{1,17},{9,25},{17,1},{25,9},{2,18},{10... | collective-permute-start | bytes 1179656 | tf_op jit(solution)/shard_map/ppermute | solution.py:371
  26.1 2.7 %sums.4 = (f32[256,768]{1,0:T(8,128)S(1)}, f32[64,768]{1,0:T(8,128)S(1)}, f32[64,768]{1,0:T(8,128)S(1)}, f32[64,768]{1,0:T(8,128)S(1)}, f32[64,768]{1,0:T(8,128)...) custom-call(f32[2,2048]{1,0:T(2,128)S(1)} %pad_maximum_fusion.stats_ref, ...), custom_call_target="tpu_custom_call" | custom-call | flops 1 | bytes 1 | tf_op jit(solution)/shard_map/sums/pallas_call | solution.py:247
  32.2 1.5 %collective-permute-start.12 = (f32[128,768]{1,0:T(8,128)S(1)}, f32[128,768]{1,0:T(8,128)S(1)}, u32[]{:S(2)}, u32[]{:S(2)}) collective-permute-start(f32[128,768]{1,0:T(8,128)S(1)} %get-tuple-element.83.refs_3_), channel_id=1, source_target_pairs={{0,16},{8,24},{16,0},{24,8},{1,17},{9,25},{17,1},{25,9},{2,18},{10... | collective-permute-start | bytes 1179656 | tf_op jit(solution)/shard_map/ppermute | solution.py:371
  33.7 2.9 %collective-permute-done.6.refs_2_.refs_1_ = f32[128,768]{1,0:T(8,128)S(1)} collective-permute-done((f32[128,768]{1,0:T(8,128)S(1)}, f32[128,768]{1,0:T(8,128)S(1)}, u32[]{:S(2)}, u32[]{:S(2)}) %collective-permute-start.6) | collective-permute-done | bytes 393248 | tf_op jit(solution)/shard_map/ppermute | solution.py:371
  36.6 1.0 sums.5
  38.2 1.0 collective-permute-done.8.refs_1_
  39.5 1.5 %collective-permute-start.10 = (f32[128,768]{1,0:T(8,128)S(1)}, f32[128,768]{1,0:T(8,128)S(1)}, u32[]{:S(2)}, u32[]{:S(2)}) collective-permute-start(f32[128,768]{1,0:T(8,128)S(1)} %fold.8.refs_11_.refs_0_), channel_id=1, source_target_pairs={{0,16},{8,24},{16,0},{24,8},{1,17},{9,25},{17,1},{25,9},{2,18},{10... | collective-permute-start | bytes 1179656 | tf_op jit(solution)/shard_map/ppermute | solution.py:371
  41.1 12.9 %collective-permute-done.12.refs_4_ = f32[128,768]{1,0:T(8,128)S(1)} collective-permute-done((f32[128,768]{1,0:T(8,128)S(1)}, f32[128,768]{1,0:T(8,128)S(1)}, u32[]{:S(2)}, u32[]{:S(2)}) %collective-permute-start.12) | collective-permute-done | bytes 393248 | tf_op jit(solution)/shard_map/ppermute | solution.py:371
  57.2 3.4 %scores.3 = (f32[2,2048]{1,0:T(2,128)S(1)}, f32[256,2048]{1,0:T(8,128)S(1)}, f32[256,2048]{1,0:T(8,128)S(1)}, f32[256,2048]{1,0:T(8,128)S(1)}) custom-call(bf16[768,2048]{1,0:T(8,128)(2,1)S(1)} %get-tuple-element.62.turned_ref, f32[128,768]{1,0:T(8,128)S(1)} %get-tuple-element.86.refs_0_.refs_2_, f32[128,768]{1,0:T(8,128)S(1)} %get-tuple-element.87.refs_1_.refs_5_, ...), custom_call_target="tpu_custom_call" | custom-call | flops 1 | bytes 1 | tf_op jit(solution)/shard_map/scores/pallas_call | solution.py:168
  60.6 1.0 collective-permute-done.10.refs_1_
  61.8 0.7 scores.4
  62.5 1.0 collective-permute-done.17.refs_0_
  63.5 0.7 scores.5
  64.3 10.0 %all_to_all.11 = f32[8,2,2048]{2,1,0:T(2,128)S(1)} all-to-all(f32[8,2,2048]{2,1,0:T(2,128)S(1)} %broadcast_in_dim.8), channel_id=1, replica_groups=mesh['dp'=4,'cent'=8] {'cent'}, dimensions={0} | all-to-all | bytes 262144 | tf_op jit(solution)/shard_map/all_to_all | solution.py:359
  74.5 0.6 side_sums.6.refs_0_
  75.2 0.6 side_sums.7.mine_ref
  75.8 1.1 collective-permute-done.18.refs_0_
  76.9 1.6 %collective-permute-start.24 = (f32[128,768]{1,0:T(8,128)S(1)}, f32[128,768]{1,0:T(8,128)S(1)}, u32[]{:S(2)}, u32[]{:S(2)}) collective-permute-start(f32[128,768]{1,0:T(8,128)S(1)} %fold.9.refs_5_.refs_0_), channel_id=1, source_target_pairs={{0,16},{8,24},{16,0},{24,8},{1,17},{9,25},{17,1},{25,9},{2,18},{10... | collective-permute-start | bytes 1179656 | tf_op jit(solution)/shard_map/ppermute | solution.py:371
  78.5 2.7 %sums.6 = (f32[256,768]{1,0:T(8,128)S(1)}, f32[64,768]{1,0:T(8,128)S(1)}, f32[64,768]{1,0:T(8,128)S(1)}, f32[64,768]{1,0:T(8,128)S(1)}, f32[64,768]{1,0:T(8,128)...) custom-call(f32[2,2048]{1,0:T(2,128)S(1)} %pad_maximum_fusion.1.stats_ref, ...), custom_call_target="tpu_custom_call" | custom-call | flops 1 | bytes 1 | tf_op jit(solution)/shard_map/sums/pallas_call | solution.py:247
  84.6 1.5 %collective-permute-start.30 = (f32[128,768]{1,0:T(8,128)S(1)}, f32[128,768]{1,0:T(8,128)S(1)}, u32[]{:S(2)}, u32[]{:S(2)}) collective-permute-start(f32[128,768]{1,0:T(8,128)S(1)} %get-tuple-element.115.refs_3_), channel_id=1, source_target_pairs={{0,16},{8,24},{16,0},{24,8},{1,17},{9,25},{17,1},{25,9},{2,18},{10... | collective-permute-start | bytes 1179656 | tf_op jit(solution)/shard_map/ppermute | solution.py:371
  86.1 2.9 %collective-permute-done.24.refs_3_.refs_1_ = f32[128,768]{1,0:T(8,128)S(1)} collective-permute-done((f32[128,768]{1,0:T(8,128)S(1)}, f32[128,768]{1,0:T(8,128)S(1)}, u32[]{:S(2)}, u32[]{:S(2)}) %collective-permute-start.24) | collective-permute-done | bytes 393248 | tf_op jit(solution)/shard_map/ppermute | solution.py:371
  88.9 1.0 sums.7
  90.6 1.0 collective-permute-done.26.refs_1_
  91.9 1.6 %collective-permute-start.28 = (f32[128,768]{1,0:T(8,128)S(1)}, f32[128,768]{1,0:T(8,128)S(1)}, u32[]{:S(2)}, u32[]{:S(2)}) collective-permute-start(f32[128,768]{1,0:T(8,128)S(1)} %fold.11.refs_11_.refs_0_), channel_id=1, source_target_pairs={{0,16},{8,24},{16,0},{24,8},{1,17},{9,25},{17,1},{25,9},{2,18},{10... | collective-permute-start | bytes 1179656 | tf_op jit(solution)/shard_map/ppermute | solution.py:371
  93.5 12.8 %collective-permute-done.30.refs_4_ = f32[128,768]{1,0:T(8,128)S(1)} collective-permute-done((f32[128,768]{1,0:T(8,128)S(1)}, f32[128,768]{1,0:T(8,128)S(1)}, u32[]{:S(2)}, u32[]{:S(2)}) %collective-permute-start.30) | collective-permute-done | bytes 393248 | tf_op jit(solution)/shard_map/ppermute | solution.py:371
  109.7 2.6 %place.2 = (f32[1024,768]{1,0:T(8,128)}, f32[8,128]{1,0:T(8,128)S(1)}) custom-call(s32[2]{0:T(128)S(1)} %pad_add_fusion.at_ref, f32[96,768]{1,0:T(8,128)S(1)} %get-tuple-element.116.refs_0_, f32[96,768]{1,0:T(8,128)S(1)} %get-tuple-element.117.refs_1_, f32[96,768]{1,0:T(8,128)S(1)} %get-tuple-element.118.refs_2_, f32[96,768]{1,0:T(8,128)S(1)} %get-tuple-element.119.refs_3_, ...), custom_call_target="tpu_custom_call" | custom-call | flops 1 | bytes 1 | tf_op jit(solution)/shard_map/place/pallas_call | solution.py:349
  112.3 1.7 %collective-permute-done.28.refs_1_ = f32[128,768]{1,0:T(8,128)S(1)} collective-permute-done((f32[128,768]{1,0:T(8,128)S(1)}, f32[128,768]{1,0:T(8,128)S(1)}, u32[]{:S(2)}, u32[]{:S(2)}) %collective-permute-start.28) | collective-permute-done | bytes 393248 | tf_op jit(solution)/shard_map/ppermute | solution.py:371
  114.1 1.7 %collective-permute-done.35.refs_1_ = f32[128,768]{1,0:T(8,128)S(1)} collective-permute-done((f32[128,768]{1,0:T(8,128)S(1)}, f32[128,768]{1,0:T(8,128)S(1)}, u32[]{:S(2)}, u32[]{:S(2)}) %collective-permute-start.35) | collective-permute-done | bytes 393248 | tf_op jit(solution)/shard_map/ppermute | solution.py:370
  115.9 1.4 %place.3 = f32[1024,768]{1,0:T(8,128)} custom-call(s32[2]{0:T(128)S(1)} %pad_add_fusion.at_ref, f32[128,768]{1,0:T(8,128)S(1)} %update.7.refs_0_, f32[128,768]{1,0:T(8,128)S(1)} %collective-permute-done.35.refs_1_, f32[1024,768]{1,0:T(8,128)} %get-tuple-element.121.refs_2_), custom_call_target="tpu_custom_call", output_to_operand_aliasing={{}: (3, {})} | custom-call | flops 1 | bytes 1 | tf_op jit(solution)/shard_map/place/pallas_call | solution.py:349
  (78 shorter events, 17.6 us)
Async XLA Ops:
  22.7 1.8 %collective-permute-start = (f32[128,768]{1,0:T(8,128)S(1)}, f32[128,768]{1,0:T(8,128)S(1)}, u32[]{:S(2)}, u32[]{:S(2)}) collective-permute-start(f32[128,768]{1,0:T(8,128)S(1)} %side_sums.4.refs_0_), channel_id=1, source_target_pairs={{0,8},{8,0},{16,24},{24,16},{1,9},{9,1},{17,25},{25,17},{2,10},{10... | collective-permute-start | bytes 1179656 | tf_op jit(solution)/shard_map/ppermute | solution.py:370
  24.6 12.0 %collective-permute-start.6 = (f32[128,768]{1,0:T(8,128)S(1)}, f32[128,768]{1,0:T(8,128)S(1)}, u32[]{:S(2)}, u32[]{:S(2)}) collective-permute-start(f32[128,768]{1,0:T(8,128)S(1)} %fold.6.refs_4_.refs_0_), channel_id=1, source_target_pairs={{0,16},{8,24},{16,0},{24,8},{1,17},{9,25},{17,1},{25,9},{2,18},{10... | collective-permute-start | bytes 1179656 | tf_op jit(solution)/shard_map/ppermute | solution.py:371
  28.9 1.6 %collective-permute-start.1 = (f32[64,768]{1,0:T(8,128)S(1)}, f32[64,768]{1,0:T(8,128)S(1)}, u32[]{:S(2)}, u32[]{:S(2)}) collective-permute-start(f32[64,768]{1,0:T(8,128)S(1)} %get-tuple-element.70), channel_id=1, source_target_pairs={{0,8},{8,0},{16,24},{24,16},{1,9},{9,1},{17,25},{25,17},{2,10},{10... | collective-permute-start | bytes 589832 | tf_op jit(solution)/shard_map/ppermute | solution.py:370
  29.4 1.4 %collective-permute-start.2 = (f32[64,768]{1,0:T(8,128)S(1)}, f32[64,768]{1,0:T(8,128)S(1)}, u32[]{:S(2)}, u32[]{:S(2)}) collective-permute-start(f32[64,768]{1,0:T(8,128)S(1)} %get-tuple-element.71), channel_id=1, source_target_pairs={{0,8},{8,0},{16,24},{24,16},{1,9},{9,1},{17,25},{25,17},{2,10},{10... | collective-permute-start | bytes 589832 | tf_op jit(solution)/shard_map/ppermute | solution.py:370
  29.5 1.6 %collective-permute-start.3 = (f32[64,768]{1,0:T(8,128)S(1)}, f32[64,768]{1,0:T(8,128)S(1)}, u32[]{:S(2)}, u32[]{:S(2)}) collective-permute-start(f32[64,768]{1,0:T(8,128)S(1)} %get-tuple-element.72), channel_id=1, source_target_pairs={{0,8},{8,0},{16,24},{24,16},{1,9},{9,1},{17,25},{25,17},{2,10},{10... | collective-permute-start | bytes 589832 | tf_op jit(solution)/shard_map/ppermute | solution.py:370
  30.0 1.4 %collective-permute-start.4 = (f32[64,768]{1,0:T(8,128)S(1)}, f32[64,768]{1,0:T(8,128)S(1)}, u32[]{:S(2)}, u32[]{:S(2)}) collective-permute-start(f32[64,768]{1,0:T(8,128)S(1)} %get-tuple-element.73), channel_id=1, source_target_pairs={{0,8},{8,0},{16,24},{24,16},{1,9},{9,1},{17,25},{25,17},{2,10},{10... | collective-permute-start | bytes 589832 | tf_op jit(solution)/shard_map/ppermute | solution.py:370
  31.6 22.4 %collective-permute-start.11 = (f32[136,768]{1,0:T(8,128)S(1)}, f32[136,768]{1,0:T(8,128)S(1)}, u32[]{:S(2)}, u32[]{:S(2)}) collective-permute-start(f32[136,768]{1,0:T(8,128)S(1)} %get-tuple-element.76.refs_1_.refs_6_.refs_9_.refs_3_), channel_id=1, source_target_pairs={{0,16},{8,24},{16,0},{24,8},{1,17},{9,25},{17,1},{25,9},{2,18},{10... | collective-permute-start | bytes 1253384 | tf_op jit(solution)/shard_map/ppermute | solution.py:371
  32.2 21.7 %collective-permute-start.12 = (f32[128,768]{1,0:T(8,128)S(1)}, f32[128,768]{1,0:T(8,128)S(1)}, u32[]{:S(2)}, u32[]{:S(2)}) collective-permute-start(f32[128,768]{1,0:T(8,128)S(1)} %get-tuple-element.83.refs_3_), channel_id=1, source_target_pairs={{0,16},{8,24},{16,0},{24,8},{1,17},{9,25},{17,1},{25,9},{2,18},{10... | collective-permute-start | bytes 1179656 | tf_op jit(solution)/shard_map/ppermute | solution.py:371
  37.6 1.9 %collective-permute-start.7 = (f32[48,768]{1,0:T(8,128)S(1)}, f32[48,768]{1,0:T(8,128)S(1)}, u32[]{:S(2)}, u32[]{:S(2)}) collective-permute-start(f32[48,768]{1,0:T(8,128)S(1)} %get-tuple-element.78), channel_id=1, source_target_pairs={{0,8},{8,0},{16,24},{24,16},{1,9},{9,1},{17,25},{25,17},{2,10},{10... | collective-permute-start | bytes 442376 | tf_op jit(solution)/shard_map/ppermute | solution.py:370
  37.7 1.5 %collective-permute-start.8 = (f32[40,768]{1,0:T(8,128)S(1)}, f32[40,768]{1,0:T(8,128)S(1)}, u32[]{:S(2)}, u32[]{:S(2)}) collective-permute-start(f32[40,768]{1,0:T(8,128)S(1)} %get-tuple-element.79), channel_id=1, source_target_pairs={{0,8},{8,0},{16,24},{24,16},{1,9},{9,1},{17,25},{25,17},{2,10},{10... | collective-permute-start | bytes 368648 | tf_op jit(solution)/shard_map/ppermute | solution.py:370
  39.5 22.0 %collective-permute-start.10 = (f32[128,768]{1,0:T(8,128)S(1)}, f32[128,768]{1,0:T(8,128)S(1)}, u32[]{:S(2)}, u32[]{:S(2)}) collective-permute-start(f32[128,768]{1,0:T(8,128)S(1)} %fold.8.refs_11_.refs_0_), channel_id=1, source_target_pairs={{0,16},{8,24},{16,0},{24,8},{1,17},{9,25},{17,1},{25,9},{2,18},{10... | collective-permute-start | bytes 1179656 | tf_op jit(solution)/shard_map/ppermute | solution.py:371
  54.3 1.6 %collective-permute-start.13 = (f32[96,768]{1,0:T(8,128)S(1)}, f32[96,768]{1,0:T(8,128)S(1)}, u32[]{:S(2)}, u32[]{:S(2)}) collective-permute-start(f32[96,768]{1,0:T(8,128)S(1)} %get-tuple-element.89), channel_id=1, source_target_pairs={{0,8},{8,0},{16,24},{24,16},{1,9},{9,1},{17,25},{25,17},{2,10},{10... | collective-permute-start | bytes 884744 | tf_op jit(solution)/shard_map/ppermute | solution.py:370
  54.4 2.0 %collective-permute-start.14 = (f32[96,768]{1,0:T(8,128)S(1)}, f32[96,768]{1,0:T(8,128)S(1)}, u32[]{:S(2)}, u32[]{:S(2)}) collective-permute-start(f32[96,768]{1,0:T(8,128)S(1)} %get-tuple-element.90), channel_id=1, source_target_pairs={{0,8},{8,0},{16,24},{24,16},{1,9},{9,1},{17,25},{25,17},{2,10},{10... | collective-permute-start | bytes 884744 | tf_op jit(solution)/shard_map/ppermute | solution.py:370
  54.9 1.9 %collective-permute-start.15 = (f32[96,768]{1,0:T(8,128)S(1)}, f32[96,768]{1,0:T(8,128)S(1)}, u32[]{:S(2)}, u32[]{:S(2)}) collective-permute-start(f32[96,768]{1,0:T(8,128)S(1)} %get-tuple-element.91), channel_id=1, source_target_pairs={{0,8},{8,0},{16,24},{24,16},{1,9},{9,1},{17,25},{25,17},{2,10},{10... | collective-permute-start | bytes 884744 | tf_op jit(solution)/shard_map/ppermute | solution.py:370
  54.9 2.3 %collective-permute-start.16 = (f32[96,768]{1,0:T(8,128)S(1)}, f32[96,768]{1,0:T(8,128)S(1)}, u32[]{:S(2)}, u32[]{:S(2)}) collective-permute-start(f32[96,768]{1,0:T(8,128)S(1)} %get-tuple-element.92), channel_id=1, source_target_pairs={{0,8},{8,0},{16,24},{24,16},{1,9},{9,1},{17,25},{25,17},{2,10},{10... | collective-permute-start | bytes 884744 | tf_op jit(solution)/shard_map/ppermute | solution.py:370
  61.7 1.8 %collective-permute-start.17 = (f32[128,768]{1,0:T(8,128)S(1)}, f32[128,768]{1,0:T(8,128)S(1)}, u32[]{:S(2)}, u32[]{:S(2)}) collective-permute-start(f32[128,768]{1,0:T(8,128)S(1)} %get-tuple-element.94), channel_id=1, source_target_pairs={{0,8},{8,0},{16,24},{24,16},{1,9},{9,1},{17,25},{25,17},{2,10},{10... | collective-permute-start | bytes 1179656 | tf_op jit(solution)/shard_map/ppermute | solution.py:370
  75.1 1.8 %collective-permute-start.18 = (f32[128,768]{1,0:T(8,128)S(1)}, f32[128,768]{1,0:T(8,128)S(1)}, u32[]{:S(2)}, u32[]{:S(2)}) collective-permute-start(f32[128,768]{1,0:T(8,128)S(1)} %side_sums.6.refs_0_), channel_id=1, source_target_pairs={{0,8},{8,0},{16,24},{24,16},{1,9},{9,1},{17,25},{25,17},{2,10},{10... | collective-permute-start | bytes 1179656 | tf_op jit(solution)/shard_map/ppermute | solution.py:370
  76.9 12.0 %collective-permute-start.24 = (f32[128,768]{1,0:T(8,128)S(1)}, f32[128,768]{1,0:T(8,128)S(1)}, u32[]{:S(2)}, u32[]{:S(2)}) collective-permute-start(f32[128,768]{1,0:T(8,128)S(1)} %fold.9.refs_5_.refs_0_), channel_id=1, source_target_pairs={{0,16},{8,24},{16,0},{24,8},{1,17},{9,25},{17,1},{25,9},{2,18},{10... | collective-permute-start | bytes 1179656 | tf_op jit(solution)/shard_map/ppermute | solution.py:371
  81.3 1.6 %collective-permute-start.19 = (f32[64,768]{1,0:T(8,128)S(1)}, f32[64,768]{1,0:T(8,128)S(1)}, u32[]{:S(2)}, u32[]{:S(2)}) collective-permute-start(f32[64,768]{1,0:T(8,128)S(1)} %get-tuple-element.104), channel_id=1, source_target_pairs={{0,8},{8,0},{16,24},{24,16},{1,9},{9,1},{17,25},{25,17},{2,10},{10... | collective-permute-start | bytes 589832 | tf_op jit(solution)/shard_map/ppermute | solution.py:370
  81.8 1.4 %collective-permute-start.20 = (f32[64,768]{1,0:T(8,128)S(1)}, f32[64,768]{1,0:T(8,128)S(1)}, u32[]{:S(2)}, u32[]{:S(2)}) collective-permute-start(f32[64,768]{1,0:T(8,128)S(1)} %get-tuple-element.105), channel_id=1, source_target_pairs={{0,8},{8,0},{16,24},{24,16},{1,9},{9,1},{17,25},{25,17},{2,10},{10... | collective-permute-start | bytes 589832 | tf_op jit(solution)/shard_map/ppermute | solution.py:370
  81.9 1.6 %collective-permute-start.21 = (f32[64,768]{1,0:T(8,128)S(1)}, f32[64,768]{1,0:T(8,128)S(1)}, u32[]{:S(2)}, u32[]{:S(2)}) collective-permute-start(f32[64,768]{1,0:T(8,128)S(1)} %get-tuple-element.106), channel_id=1, source_target_pairs={{0,8},{8,0},{16,24},{24,16},{1,9},{9,1},{17,25},{25,17},{2,10},{10... | collective-permute-start | bytes 589832 | tf_op jit(solution)/shard_map/ppermute | solution.py:370
  82.4 1.4 %collective-permute-start.22 = (f32[64,768]{1,0:T(8,128)S(1)}, f32[64,768]{1,0:T(8,128)S(1)}, u32[]{:S(2)}, u32[]{:S(2)}) collective-permute-start(f32[64,768]{1,0:T(8,128)S(1)} %get-tuple-element.107), channel_id=1, source_target_pairs={{0,8},{8,0},{16,24},{24,16},{1,9},{9,1},{17,25},{25,17},{2,10},{10... | collective-permute-start | bytes 589832 | tf_op jit(solution)/shard_map/ppermute | solution.py:370
  84.0 22.3 %collective-permute-start.29 = (f32[136,768]{1,0:T(8,128)S(1)}, f32[136,768]{1,0:T(8,128)S(1)}, u32[]{:S(2)}, u32[]{:S(2)}) collective-permute-start(f32[136,768]{1,0:T(8,128)S(1)} %get-tuple-element.110.refs_2_.refs_6_.refs_9_.refs_3_), channel_id=1, source_target_pairs={{0,16},{8,24},{16,0},{24,8},{1,17},{9,25},{17,1},{25,9},{2,18},{10... | collective-permute-start | bytes 1253384 | tf_op jit(solution)/shard_map/ppermute | solution.py:371
  84.6 21.7 %collective-permute-start.30 = (f32[128,768]{1,0:T(8,128)S(1)}, f32[128,768]{1,0:T(8,128)S(1)}, u32[]{:S(2)}, u32[]{:S(2)}) collective-permute-start(f32[128,768]{1,0:T(8,128)S(1)} %get-tuple-element.115.refs_3_), channel_id=1, source_target_pairs={{0,16},{8,24},{16,0},{24,8},{1,17},{9,25},{17,1},{25,9},{2,18},{10... | collective-permute-start | bytes 1179656 | tf_op jit(solution)/shard_map/ppermute | solution.py:371
  90.0 1.9 %collective-permute-start.25 = (f32[48,768]{1,0:T(8,128)S(1)}, f32[48,768]{1,0:T(8,128)S(1)}, u32[]{:S(2)}, u32[]{:S(2)}) collective-permute-start(f32[48,768]{1,0:T(8,128)S(1)} %get-tuple-element.112), channel_id=1, source_target_pairs={{0,8},{8,0},{16,24},{24,16},{1,9},{9,1},{17,25},{25,17},{2,10},{10... | collective-permute-start | bytes 442376 | tf_op jit(solution)/shard_map/ppermute | solution.py:370
  90.0 1.5 %collective-permute-start.26 = (f32[40,768]{1,0:T(8,128)S(1)}, f32[40,768]{1,0:T(8,128)S(1)}, u32[]{:S(2)}, u32[]{:S(2)}) collective-permute-start(f32[40,768]{1,0:T(8,128)S(1)} %get-tuple-element.113), channel_id=1, source_target_pairs={{0,8},{8,0},{16,24},{24,16},{1,9},{9,1},{17,25},{25,17},{2,10},{10... | collective-permute-start | bytes 368648 | tf_op jit(solution)/shard_map/ppermute | solution.py:370
  91.9 22.0 %collective-permute-start.28 = (f32[128,768]{1,0:T(8,128)S(1)}, f32[128,768]{1,0:T(8,128)S(1)}, u32[]{:S(2)}, u32[]{:S(2)}) collective-permute-start(f32[128,768]{1,0:T(8,128)S(1)} %fold.11.refs_11_.refs_0_), channel_id=1, source_target_pairs={{0,16},{8,24},{16,0},{24,8},{1,17},{9,25},{17,1},{25,9},{2,18},{10... | collective-permute-start | bytes 1179656 | tf_op jit(solution)/shard_map/ppermute | solution.py:371
  106.6 1.6 %collective-permute-start.31 = (f32[96,768]{1,0:T(8,128)S(1)}, f32[96,768]{1,0:T(8,128)S(1)}, u32[]{:S(2)}, u32[]{:S(2)}) collective-permute-start(f32[96,768]{1,0:T(8,128)S(1)} %get-tuple-element.116.refs_0_), channel_id=1, source_target_pairs={{0,8},{8,0},{16,24},{24,16},{1,9},{9,1},{17,25},{25,17},{2,10},{10... | collective-permute-start | bytes 884744 | tf_op jit(solution)/shard_map/ppermute | solution.py:370
  106.7 2.1 %collective-permute-start.32 = (f32[96,768]{1,0:T(8,128)S(1)}, f32[96,768]{1,0:T(8,128)}, u32[]{:S(2)}, u32[]{:S(2)}) collective-permute-start(f32[96,768]{1,0:T(8,128)S(1)} %get-tuple-element.117.refs_1_), channel_id=1, source_target_pairs={{0,8},{8,0},{16,24},{24,16},{1,9},{9,1},{17,25},{25,17},{2,10},{10... | collective-permute-start | bytes 884744 | tf_op jit(solution)/shard_map/ppermute | solution.py:370
  107.2 2.0 %collective-permute-start.33 = (f32[96,768]{1,0:T(8,128)S(1)}, f32[96,768]{1,0:T(8,128)}, u32[]{:S(2)}, u32[]{:S(2)}) collective-permute-start(f32[96,768]{1,0:T(8,128)S(1)} %get-tuple-element.118.refs_2_), channel_id=1, source_target_pairs={{0,8},{8,0},{16,24},{24,16},{1,9},{9,1},{17,25},{25,17},{2,10},{10... | collective-permute-start | bytes 884744 | tf_op jit(solution)/shard_map/ppermute | solution.py:370
  107.3 2.4 %collective-permute-start.34 = (f32[96,768]{1,0:T(8,128)S(1)}, f32[96,768]{1,0:T(8,128)}, u32[]{:S(2)}, u32[]{:S(2)}) collective-permute-start(f32[96,768]{1,0:T(8,128)S(1)} %get-tuple-element.119.refs_3_), channel_id=1, source_target_pairs={{0,8},{8,0},{16,24},{24,16},{1,9},{9,1},{17,25},{25,17},{2,10},{10... | collective-permute-start | bytes 884744 | tf_op jit(solution)/shard_map/ppermute | solution.py:370
  114.1 1.8 %collective-permute-start.35 = (f32[128,768]{1,0:T(8,128)S(1)}, f32[128,768]{1,0:T(8,128)S(1)}, u32[]{:S(2)}, u32[]{:S(2)}) collective-permute-start(f32[128,768]{1,0:T(8,128)S(1)} %update.7.refs_0_), channel_id=1, source_target_pairs={{0,8},{8,0},{16,24},{24,16},{1,9},{9,1},{17,25},{25,17},{2,10},{10... | collective-permute-start | bytes 1179656 | tf_op jit(solution)/shard_map/ppermute | solution.py:370
  (5 other events, 18.2 us)
